TPU v7x, 32 devices: a whole 2x2x4 slice. The times are simulated.
32 devices in a mesh: rep: 2 (over x), section: 2 (over core), tp: 8 (over z, y).
Axes of the slice: x: 2, y: 2, z: 4, core: 2. Of those that a mesh axis runs over, the one named last changes fastest.
Arguments:
- queries: bfloat16 [2, 16, 64, 128], P('section', 'rep', 'tp'), parts along dimension 1, may hold values from -200 to 200
- new_kv: bfloat16 [2, 16, 2, 4, 128], P('section', 'rep'), parts along dimension 1, may hold values from -6 to 6
- kv_cache: bfloat16 [2, 16, 2, 4, 1024, 128], P('section', 'rep', None, None, 'tp'), parts along dimension 1, may hold values from -6 to 6
- lengths: int32 [2, 16], P('section', 'rep'), parts along dimension 1, may hold values from 2 to 1023, as said below
- residual: bfloat16 [2, 16, 16384], P('section', 'rep', 'tp'), parts along dimension 1, may hold values from -3 to 3
- out_weight: bfloat16 [2, 8192, 16384], P('section', 'tp'), may hold values from -0.09375 to 0.09375
Outputs:
- handed: bfloat16 [2, 16, 16384], P('section', 'rep'), parts along dimension 1
There are 2 independent parts, one for each index of `rep`. A program takes and returns all parts, laid end to end along the dimension named above; an argument that names none is the same for every part. Nothing has to cross between parts.
Inputs may be any that keep to these rules, and one draw needn't show every extreme that they name: Row r attends to cached positions 0 to lengths - 1 and to its new token at position lengths; in each section some row has the largest value.
All inputs are finite; a program needn't handle non-finite values.
Results may differ from a plain program's by a relative error of at most 0.039.
Values may be sent and summed in bfloat16 or wider, within the bound.
No kernel may reach another device: no remote copies, remote signals or barrier semaphores. Data moves between devices by JAX's collectives and lax.ppermute only.
A program may use at most 192 MiB of HBM per device.

v0:
```python
import math

import jax
import jax.numpy as jnp
from jax import lax
from jax.sharding import PartitionSpec as P

QB = 128


def joined(array, axis, combine):
    everything = jax.tree.map(
        lambda part, kind: lax.all_gather(part.astype(kind), axis),
        array,
        (jnp.bfloat16, jnp.bfloat16, jnp.bfloat16),
    )

    def take(k):
        return jax.tree.map(lambda part, own: part[k].astype(own.dtype), everything, array)

    return lax.fori_loop(
        1, lax.axis_size(axis), lambda k, so_far: combine(so_far, take(k)), take(0)
    )


def shifted(array, axis, by):
    peers = lax.axis_size(axis)
    return lax.ppermute(array, axis, [(i, (i + by) % peers) for i in range(peers)])


def block_scale(blocks):
    return ((jnp.max(jnp.abs(blocks), axis=-1) + 1e-06) / 127.0).astype(jnp.bfloat16)


def quantize(blocks, scale_wide):
    return jnp.clip(jnp.floor(blocks / scale_wide[..., None] + 0.5), -127.0, 127.0).astype(
        jnp.bfloat16
    )


def join_parts(earlier, later):
    overall = jnp.maximum(earlier[0], later[0])
    factor_one = jnp.exp(earlier[0] - overall)
    factor_two = jnp.exp(later[0] - overall)
    totals = earlier[1] * factor_one + later[1] * factor_two
    mixed = earlier[2] * factor_one[..., None] + later[2] * factor_two[..., None]
    return (overall, totals, mixed)


def local(queries, new_kv, kv_cache, lengths, residual, out_weight):
    tp_size = lax.axis_size("tp")
    tp_rank = lax.axis_index("tp")
    row_count = queries.shape[1]
    heads_dev = queries.shape[2]
    head_dim = queries.shape[3]
    kv_heads = kv_cache.shape[3]
    local_span = kv_cache.shape[4]
    all_queries = lax.all_gather(queries, "tp", axis=2, tiled=True)[0]
    head_count = all_queries.shape[1]
    group_size = head_count // kv_heads
    length = lengths[0]
    position = tp_rank * local_span + jnp.arange(local_span, dtype=jnp.int32)
    written = position[None, :] == length[:, None]
    stored = jnp.where(written[:, None, None, :, None], new_kv[0][:, :, :, None, :], kv_cache[0])
    key_block = stored[:, 0]
    value_block = stored[:, 1]
    grouped = all_queries.reshape(row_count, kv_heads, group_size, head_dim)
    scores = jnp.einsum("rkgd,rkpd->rkgp", grouped, key_block, preferred_element_type=jnp.float32)
    scores = scores * (1.0 / math.sqrt(head_dim))
    visible = (position[None, :] <= length[:, None])[:, None, None, :]
    scores = jnp.where(visible, scores, -1e30)
    top_score = jnp.max(scores, axis=-1)
    weights = jnp.where(visible, jnp.exp(scores - top_score[..., None]), 0.0)
    totals = jnp.sum(weights, axis=-1)
    mixed = jnp.einsum(
        "rkgp,rkpd->rkgd",
        weights.astype(jnp.bfloat16),
        value_block,
        preferred_element_type=jnp.float32,
    )
    top_score = top_score.reshape(row_count, head_count)
    totals = totals.reshape(row_count, head_count)
    mixed = mixed.reshape(row_count, head_count, head_dim)
    top_score, totals, mixed = joined((top_score, totals, mixed), "tp", join_parts)
    attended = mixed / totals[..., None]
    own_heads = lax.dynamic_slice_in_dim(attended, tp_rank * heads_dev, heads_dev, 1)
    flattened = own_heads.astype(jnp.bfloat16).reshape(row_count, heads_dev * head_dim)
    partial_out = jnp.dot(flattened, out_weight[0], preferred_element_type=jnp.float32)
    full_width = partial_out.shape[1]
    blocks_dev = full_width // (tp_size * QB)
    blocks = partial_out.reshape(row_count, tp_size, blocks_dev, QB)
    scales = block_scale(blocks)
    scale_wide = lax.optimization_barrier(scales).astype(jnp.float32)
    levels = quantize(blocks, scale_wide)
    got_levels, got_scales = (
        lax.all_to_all(levels, "tp", split_axis=1, concat_axis=1, tiled=True),
        lax.all_to_all(scales, "tp", split_axis=1, concat_axis=1, tiled=True),
    )
    summed = jnp.sum(
        got_levels.astype(jnp.float32) * got_scales.astype(jnp.float32)[..., None], axis=1
    )
    summed = residual[0].astype(jnp.float32).reshape(row_count, blocks_dev, QB) + summed
    scales_out = block_scale(summed)
    scales_out_wide = lax.optimization_barrier(scales_out).astype(jnp.float32)
    levels_out = quantize(summed, scales_out_wide)
    full_levels, full_scales = (
        lax.all_gather(levels_out, "tp", axis=1, tiled=True),
        lax.all_gather(scales_out, "tp", axis=1, tiled=True),
    )
    restored_out = full_levels.astype(jnp.float32) * full_scales.astype(jnp.float32)[..., None]
    output = restored_out.astype(jnp.bfloat16).reshape(1, row_count, full_width)
    return shifted(output, "section", 1)


def solution(mesh):
    return jax.shard_map(
        local,
        mesh=mesh,
        in_specs=(
            P("section", "rep", "tp", None),
            P("section", "rep", None, None, None),
            P("section", "rep", None, None, "tp", None),
            P("section", "rep"),
            P("section", "rep", "tp"),
            P("section", "tp", None),
        ),
        out_specs=P("section", "rep", None),
        check_vma=False,
    )
```

profile of v0, /device:TPU:0, one launch (start us, length us, event | category | flops | bytes accessed | tf_op | source)
XLA Modules:
  0.0 249.1 jit_solution(16131004182945522275)
XLA Ops:
  6.5 28.2 %all_gather.21 = bf16[1,8,64,128]{3,2,1,0:T(8,128)(2,1)S(1)} all-gather(bf16[1,8,8,128]{3,2,1,0:T(8,128)(2,1)} %param.8), channel_id=1, replica_groups=mesh['rep'=2,'section'=2,'tp'=8] {'tp'}, dimensions={2}, use_global_device_ids=true | all-gather | bytes 147456 | tf_op jit(solution)/shard_map/all_gather | solution.py:58
  35.5 2.4 bitcast_select_fusion
  38.7 1.1 convolution_convert_fusion
  40.3 44.0 %copy.34 = bf16[16384,1024]{1,0:T(8,128)(2,1)} copy(bf16[16384,1024]{0,1:T(8,128)(2,1)} %bitcast.74) | data formatting | bytes 67108864 | tf_op jit(solution)/shard_map/dot_general | solution.py:88
  84.3 26.0 %all_gather.23 = bf16[8,8,64]{2,1,0:T(8,128)(2,1)S(1)} all-gather(bf16[1,8,64]{2,1,0:T(8,128)(2,1)S(1)} %convert_element_type.153), channel_id=1, replica_groups=mesh['rep'=2,'section'=2,'tp'=8] {'tp'}, dimensions={0}, use_global_device_ids=true | all-gather | bytes 9216 | tf_op jit(solution)/shard_map/all_gather | solution.py:13
  110.3 26.0 %all_gather.22 = bf16[8,8,64]{2,1,0:T(8,128)(2,1)S(1)} all-gather(bf16[1,8,64]{2,1,0:T(8,128)(2,1)S(1)} %convert_element_type.149), channel_id=1, replica_groups=mesh['rep'=2,'section'=2,'tp'=8] {'tp'}, dimensions={0}, use_global_device_ids=true | all-gather | bytes 9216 | tf_op jit(solution)/shard_map/all_gather | solution.py:13
  136.3 0.9 fusion.9
  137.2 8.6 %while.19 = (s32[]{:T(128)}, f32[8,64]{1,0:T(8,128)S(1)}, f32[8,64]{1,0:T(8,128)S(1)}, f32[8,64,128]{2,1,0:T(8,128)S(1)}, bf16[8,8,64]{2,1,0:T(8,128)(2,1)S(1)},...) while((s32[]{:T(128)}, f32[8,64]{1,0:T(8,128)S(1)}, ...), condition=%wide.region_3.4_spmd, body=%wide.region_2.3_spmd.sunk | while | flops 266245 | bytes 673935 | solution.py:21
  137.3 1.2 fusion.29
  138.5 1.2 fusion.29
  139.7 1.2 fusion.29
  141.0 1.2 fusion.29
  142.2 1.2 fusion.29
  143.4 1.2 fusion.29
  144.6 1.2 fusion.29
  146.0 14.1 %abs_reduce_fusion = (f32[8,8,16]{0,2,1:T(8,128)S(1)}, f32[8,8,16,128]{3,0,2,1:T(8,128)S(1)}) fusion(bf16[8,16,128,1024]{3,2,1,0:T(8,128)(2,1)} %bitcast.73, bf16[8,1024,1,1]{1,0,2,3:T(8,128)(2,1)S(1)} %reshape.143), kind=kOutput, calls=%fused_computation.18 | convolution fusion | flops 268696576 | bytes 34099200 | tf_op jit(solution)/shard_map/dot_general | solution.py:88
  160.8 3.3 %all-to-all-start.1 = ((bf16[8,8,16]{2,0,1:T(8,128)(2,1)}), bf16[8,8,16]{2,0,1:T(8,128)(2,1)S(1)}, u32[]{:S(2)}, u32[]{:S(2)}) async-start(bf16[8,8,16]{2,0,1:T(8,128)(2,1)} %copy.28), calls=%async_computation.1 | async-start | bytes 32768 | tf_op jit(solution)/shard_map/all_to_all | solution.py:97
  164.2 0.9 clamp_convert_fusion
  165.1 5.6 %all-to-all-done.1 = bf16[8,8,16]{2,0,1:T(8,128)(2,1)S(1)} async-done(((bf16[8,8,16]{2,0,1:T(8,128)(2,1)}), bf16[8,8,16]{2,0,1:T(8,128)(2,1)S(1)}, u32[]{:S(2)}, u32[]{:S(2)}) %all-to-all-start.1) | async-done | bytes 2080 | tf_op jit(solution)/shard_map/all_to_all | solution.py:97
  170.7 3.4 %all-to-all-start = ((bf16[8,8,16,128]{3,0,2,1:T(8,128)(2,1)}), bf16[8,8,16,128]{3,0,2,1:T(8,128)(2,1)S(1)}, u32[]{:S(2)}, u32[]{:S(2)}) async-start(bf16[8,8,16,128]{3,0,2,1:T(8,128)(2,1)} %clamp_convert_fusion), calls=%async_computation | async-start | bytes 524288 | tf_op jit(solution)/shard_map/all_to_all | solution.py:96
  174.2 8.1 %all-to-all-done = bf16[8,8,16,128]{3,0,2,1:T(8,128)(2,1)S(1)} async-done(((bf16[8,8,16,128]{3,0,2,1:T(8,128)(2,1)}), bf16[8,8,16,128]{3,0,2,1:T(8,128)(2,1)S(1)}, u32[]{:S(2)}, u32[]{:S(2)}) %all-to-all-start) | async-done | bytes 262176 | tf_op jit(solution)/shard_map/all_to_all | solution.py:96
  182.8 26.0 %all-gather = bf16[8,16,8]{1,2,0:T(8,128)(2,1)S(1)} all-gather(bf16[1,16,8]{1,2,0:T(8,128)(2,1)S(1)} %bitcast.78), channel_id=1, replica_groups=mesh['rep'=2,'section'=2,'tp'=8] {'tp'}, dimensions={0}, use_global_device_ids=true | all-gather | bytes 2304 | tf_op jit(solution)/shard_map/all_gather | solution.py:108
  209.0 30.7 %all_gather.25 = bf16[8,128,128]{2,0,1:T(8,128)(2,1)S(1)} all-gather(bf16[8,16,128]{2,0,1:T(8,128)(2,1)S(1)} %clamp_convert_fusion.1), channel_id=1, replica_groups=mesh['rep'=2,'section'=2,'tp'=8] {'tp'}, dimensions={1}, use_global_device_ids=true | all-gather | bytes 294912 | tf_op jit(solution)/shard_map/all_gather | solution.py:107
  240.0 1.5 collective-permute-done
  (45 shorter events, 4.7 us)
Async XLA Ops:
  6.5 29.0 %copy-start = (bf16[1,8,2,4,128]{4,3,2,1,0:T(4,128)(2,1)S(1)}, bf16[1,8,2,4,128]{4,3,2,1,0:T(4,128)(2,1)}, u32[]{:S(2)}) copy-start(bf16[1,8,2,4,128]{4,3,2,1,0:T(4,128)(2,1)} %param.9) | copy-start | bytes 49156
  6.5 129.8 %all-gather.3.cloned.1.call-start = ((), (), s32[]{:S(2)}) async-start(), calls=%async_computation.2 | async-start | bytes 1179648 | tf_op jit(solution)/shard_map/all_gather | solution.py:13
  146.0 96.2 %copy-start.1 = (bf16[1,8,2,4,128]{4,3,2,1,0:T(4,128)(2,1)S(1)}, bf16[1,8,2,4,128]{4,3,2,1,0:T(4,128)(2,1)}, u32[]{:S(2)}) copy-start(bf16[1,8,2,4,128]{4,3,2,1,0:T(4,128)(2,1)} %param.9) | copy-start | bytes 49156
  160.1 22.3 %copy-start.2 = (bf16[1,8,2048]{2,1,0:T(8,128)(2,1)S(1)}, bf16[1,8,2048]{2,1,0:T(8,128)(2,1)}, u32[]{:S(2)}) copy-start(bf16[1,8,2048]{2,1,0:T(8,128)(2,1)} %param.12) | copy-start | bytes 98308
  160.8 9.8 %all-to-all-start.1 = ((bf16[8,8,16]{2,0,1:T(8,128)(2,1)}), bf16[8,8,16]{2,0,1:T(8,128)(2,1)S(1)}, u32[]{:S(2)}, u32[]{:S(2)}) async-start(bf16[8,8,16]{2,0,1:T(8,128)(2,1)} %copy.28), calls=%async_computation.1 | async-start | bytes 32768 | tf_op jit(solution)/shard_map/all_to_all | solution.py:97
  170.7 11.6 %all-to-all-start = ((bf16[8,8,16,128]{3,0,2,1:T(8,128)(2,1)}), bf16[8,8,16,128]{3,0,2,1:T(8,128)(2,1)S(1)}, u32[]{:S(2)}, u32[]{:S(2)}) async-start(bf16[8,8,16,128]{3,0,2,1:T(8,128)(2,1)} %clamp_convert_fusion), calls=%async_computation | async-start | bytes 524288 | tf_op jit(solution)/shard_map/all_to_all | solution.py:96
  239.9 1.6 collective-permute-start
Sparse Core Ops, SparseCore 0:
  39.9 39.4 all-gather.2
where the time goes:
time: 251 us; the launch traced here: 249 us
  blocking collectives  137 us (55%)
  local copies, waits for them, and re-layouts  46 us (18%)
  matrix products  16 us (6%)
  waiting for transfers between devices  15.2 us (6%)
  other arithmetic  14.3 us (6%)
  between operations  13.5 us (5%)
  starting transfers between devices  6.79 us (3%)
    all_gather x2, blocking collectives, joined(): lax.all_gather(part.astype(kind), axis)  52 us
    dot_general x1, local copies, waits for them, and re-layouts, local(): jnp.dot(flattened, out_weight[0], preferred_element_type=jnp.float32)  44 us
    all_gather x1, blocking collectives, local(): lax.all_gather(levels_out, 'tp', axis=1, tiled=True)  30.7 us
    all_gather x1, blocking collectives, local(): all_queries = lax.all_gather(queries, 'tp', axis=2, tiled=True)[0]  28.2 us
    all_gather x1, blocking collectives, local(): lax.all_gather(scales_out, 'tp', axis=1, tiled=True)  26 us
    dot_general x1, matrix products, local(): jnp.dot(flattened, out_weight[0], preferred_element_type=jnp.float32)  14.1 us
    add x7, other arithmetic, join_parts(): earlier[2] * factor_one[..., None] + later[2] * factor_two[..., None]  8.22 us
    all_to_all x1, waiting for transfers between devices, local(): lax.all_to_all(levels, 'tp', split_axis=1, concat_axis=1, tiled=True)  8.08 us
  transfers between devices with their start and end apart: 4, of which 3 were waited for; matrix products, arithmetic and copies ran while one was open for 18% of the time, Pallas kernels for 0%

commit v1 on v0

v1 whole, which is shorter than its diff:
```python
import functools
import math

import jax
import jax.numpy as jnp
from jax import lax
from jax.experimental import pallas as pl
from jax.experimental.pallas import tpu as pltpu
from jax.sharding import PartitionSpec as P

QB = 128
LANES = 128
STAT_ROWS = 16
MIB = 1 << 20
F32 = jnp.float32
BF16 = jnp.bfloat16


def exchanged(array, k, tp, sections, shift):
    pairs = [
        (s * tp + t, ((s + shift) % sections) * tp + (t ^ k))
        for s in range(sections)
        for t in range(tp)
    ]
    return lax.ppermute(array, ("section", "tp"), pairs)


def pieces(x):
    high = x.astype(BF16).astype(F32)
    rest = x - high
    middle = rest.astype(BF16).astype(F32)
    return high, middle, rest - middle


def attention_kernel(tp, group, lengths_ref, new_ref, kv_ref, *refs):
    queries, outs = refs[:tp], refs[tp : 2 * tp]
    scores_ref, mixed_ref = refs[2 * tp :]
    rows, heads = queries[0].shape[1:3]
    kv_heads, span, dim = kv_ref.shape[3:]
    per = group // heads
    rank = lax.axis_index("tp")
    first = rank * span
    scale = 1.0 / math.sqrt(dim)
    sub = lax.broadcasted_iota(jnp.int32, (span, dim), 0)
    kv_sub = lax.broadcasted_iota(jnp.int32, (kv_heads, dim), 0)

    def cached(r, which, kv_head):
        new = new_ref[0, r, which].astype(F32)
        new = jnp.sum(jnp.where(kv_sub == kv_head, new, 0.0), axis=0, keepdims=True)
        block = kv_ref[0, r, which, kv_head]
        return jnp.where(sub == lengths_ref[0, r] - first, new, block.astype(F32)).astype(BF16)

    for m in range(kv_heads):
        kv_head = (rank // per) ^ m
        for r in range(rows):
            q = jnp.concatenate(
                [queries[m * per + i][0, r].astype(F32) for i in range(per)], axis=0
            ).astype(BF16)
            keys = cached(r, 0, kv_head)
            s = lax.dot_general(q, keys, (((1,), (1,)), ((), ())), preferred_element_type=F32)
            scores_ref[m * group : (m + 1) * group, r, :] = s * scale

    row_of = lax.broadcasted_iota(jnp.int32, (rows, span), 0)
    pos = lax.broadcasted_iota(jnp.int32, (rows, span), 1) + first
    limit = jnp.zeros((rows, span), jnp.int32)
    for r in range(rows):
        limit = jnp.where(row_of == r, lengths_ref[0, r], limit)
    visible = (pos <= limit)[None]
    scores = jnp.where(visible, scores_ref[...], -1e30)
    top = jnp.max(scores, axis=-1, keepdims=True)
    weights = jnp.where(visible, jnp.exp(scores - top), 0.0)
    total = jnp.sum(weights, axis=-1, keepdims=True)
    scores_ref[...] = weights

    for m in range(kv_heads):
        kv_head = (rank // per) ^ m
        for r in range(rows):
            w = scores_ref[m * group : (m + 1) * group, r, :].astype(BF16)
            values = cached(r, 1, kv_head)
            mixed_ref[m * group : (m + 1) * group, r, :] = jnp.dot(
                w, values, preferred_element_type=F32
            )

    n = heads * rows
    sub_n = lax.broadcasted_iota(jnp.int32, (n, LANES), 0)
    lane_n = lax.broadcasted_iota(jnp.int32, (n, LANES), 1)
    stat_sub = lax.broadcasted_iota(jnp.int32, (STAT_ROWS, LANES), 0)
    for k in range(tp):
        own = slice(k * heads, (k + 1) * heads)
        outs[k][:n, :] = mixed_ref[own].reshape(n, dim).astype(BF16)
        tops = jnp.where(lane_n == sub_n, top[own].reshape(n, 1), 0.0)
        sums = jnp.where(lane_n == sub_n + n, total[own].reshape(n, 1), 0.0)
        stats = jnp.sum(tops + sums, axis=0, keepdims=True)
        tile = jnp.zeros((STAT_ROWS, LANES), F32)
        for i, piece in enumerate(pieces(stats)):
            tile = jnp.where(stat_sub == i, piece, tile)
        outs[k][n:, :] = tile.astype(BF16)


def attended_block(blocks, rows, heads):
    n = rows * heads
    sub_n = lax.broadcasted_iota(jnp.int32, (n, LANES), 0)
    lane_n = lax.broadcasted_iota(jnp.int32, (n, LANES), 1)
    tops, sums = [], []
    for block in blocks:
        tile = block[n:, :].astype(F32)
        stats = tile[0:1] + tile[1:2] + tile[2:3]
        tops.append(jnp.sum(jnp.where(lane_n == sub_n, stats, 0.0), axis=1, keepdims=True))
        sums.append(jnp.sum(jnp.where(lane_n == sub_n + n, stats, 0.0), axis=1, keepdims=True))
    overall = functools.reduce(jnp.maximum, tops)
    total = jnp.zeros((n, 1), F32)
    mixed = jnp.zeros((n, LANES), F32)
    for block, top, part in zip(blocks, tops, sums):
        factor = jnp.exp(top - overall)
        total = total + part * factor
        mixed = mixed + block[:n, :].astype(F32) * factor
    attended = mixed / total
    return jnp.concatenate(
        [attended[h * rows : (h + 1) * rows] for h in range(heads)], axis=1
    ).astype(BF16)


def requantized(x):
    top = jnp.max(jnp.abs(x), axis=-1, keepdims=True)
    scale = ((top + 1e-06) / 127.0).astype(BF16).astype(F32)
    return jnp.clip(jnp.floor(x / scale + 0.5), -127.0, 127.0) * scale


def projection_kernel(tp, rows, heads, tile, weight_ref, *refs):
    blocks, outs = refs[:tp], refs[tp : 2 * tp]
    held, sems = refs[2 * tp :]
    rank = lax.axis_index("tp")
    width = outs[0].shape[1]
    order = list(range(tp))[::-1]

    def copy(k):
        start = pl.multiple_of((rank ^ k) * width, width)
        return pltpu.make_async_copy(
            weight_ref.at[0, :, pl.ds(start, width)], held.at[k], sems.at[k]
        )

    for k in order:
        copy(k).start()
    flat = attended_block(blocks, rows, heads)
    for k in order:
        copy(k).wait()
        for c in range(width // tile):
            part = jnp.dot(
                flat, held[k, :, c * tile : (c + 1) * tile], preferred_element_type=F32
            )
            for b in range(tile // QB):
                at = c * tile + b * QB
                outs[k][:, at : at + QB] = requantized(part[:, b * QB : (b + 1) * QB]).astype(BF16)


def sum_kernel(tp, residual_ref, *refs):
    parts, out_ref = refs[:tp], refs[tp]
    for b in range(out_ref.shape[1] // QB):
        at = slice(b * QB, (b + 1) * QB)
        x = functools.reduce(lambda a, c: a + c, [part[:, at].astype(F32) for part in parts])
        x = x + residual_ref[0, :, at].astype(F32)
        out_ref[:, at] = requantized(x).astype(BF16)


def place_kernel(tp, *refs):
    blocks, out_ref = refs[:tp], refs[tp]
    width = blocks[0].shape[1]
    rank = lax.axis_index("tp")
    for k in range(tp):
        start = pl.multiple_of((rank ^ k) * width, width)
        out_ref[0, :, pl.ds(start, width)] = blocks[k][...]


def params(mib):
    return pltpu.CompilerParams(vmem_limit_bytes=mib * MIB)


def local(tp, sections, queries, new_kv, kv_cache, lengths, residual, out_weight):
    rows, heads, dim = queries.shape[1:]
    kv_heads, span = kv_cache.shape[3:5]
    group = heads * tp // kv_heads
    depth, full = out_weight.shape[1:]
    width = full // tp
    vmem = pl.BlockSpec(memory_space=pltpu.VMEM)
    far = list(range(tp))[::-1]

    def everyone(arrays, shift):
        got = {}
        for k in far:
            same = k == 0 and shift == 0
            got[k] = arrays[k] if same else exchanged(arrays[k], k, tp, sections, shift)
        return [got[k] for k in range(tp)]

    all_queries = everyone([queries] * tp, 0)
    moved_residual = exchanged(residual, 0, tp, sections, 1)
    partial = pl.pallas_call(
        functools.partial(attention_kernel, tp, group),
        out_shape=[jax.ShapeDtypeStruct((heads * rows + STAT_ROWS, dim), BF16)] * tp,
        in_specs=[pl.BlockSpec(memory_space=pltpu.SMEM), vmem, vmem] + [vmem] * tp,
        out_specs=[vmem] * tp,
        scratch_shapes=[pltpu.VMEM((heads * tp, rows, span), F32)] * 2,
        compiler_params=params(8),
        name="attention",
    )(lengths, new_kv, kv_cache, *all_queries)
    joined = everyone(partial, 0)
    levels = pl.pallas_call(
        functools.partial(projection_kernel, tp, rows, heads, min(512, width)),
        out_shape=[jax.ShapeDtypeStruct((rows, width), BF16)] * tp,
        in_specs=[pl.BlockSpec(memory_space=pl.ANY)] + [vmem] * tp,
        out_specs=[vmem] * tp,
        scratch_shapes=[pltpu.VMEM((tp, depth, width), BF16), pltpu.SemaphoreType.DMA((tp,))],
        compiler_params=params(40),
        name="projection",
    )(out_weight, *joined)
    got = everyone(levels, 1)
    own = pl.pallas_call(
        functools.partial(sum_kernel, tp),
        out_shape=jax.ShapeDtypeStruct((rows, width), BF16),
        in_specs=[vmem] * (tp + 1),
        out_specs=vmem,
        compiler_params=params(4),
        name="owner_sum",
    )(moved_residual, *got)
    return pl.pallas_call(
        functools.partial(place_kernel, tp),
        out_shape=jax.ShapeDtypeStruct((1, rows, full), BF16),
        in_specs=[vmem] * tp,
        out_specs=vmem,
        compiler_params=params(4),
        name="placed",
    )(*everyone([own] * tp, 0))


def solution(mesh):
    return jax.shard_map(
        functools.partial(local, mesh.shape["tp"], mesh.shape["section"]),
        mesh=mesh,
        in_specs=(
            P("section", "rep", "tp", None),
            P("section", "rep", None, None, None),
            P("section", "rep", None, None, "tp", None),
            P("section", "rep"),
            P("section", "rep", "tp"),
            P("section", "tp", None),
        ),
        out_specs=P("section", "rep", None),
        check_vma=False,
    )
```

time: 251 us -> 80.8 us (0.32)
  blocking collectives: 137 us -> 0 us
  local copies, waits for them, and re-layouts: 46 us -> 3.68 us
  starting transfers between devices: 6.79 us -> 45.3 us
  matrix products: 16 us -> 0 us
  Pallas kernels: 0 us -> 14.6 us
  other arithmetic: 14.3 us -> 0 us
  between operations: 13.5 us -> 0.07 us
    all_gather x5 -> x0, blocking collectives: 137 us -> none  [the longest x2 52 us: joined(): lax.all_gather(part.astype(kind), axis)]
    ppermute x1 -> x30, starting transfers between devices: 0.07 us -> 45.3 us  [exchanged(): return lax.ppermute(array, ('section', 'tp'), pairs)]
    dot_general x1 -> x0, local copies, waits for them, and re-layouts: 44 us -> none  [local(): jnp.dot(flattened, out_weight[0], preferred_element_type=jnp.float32)]
    dot_general x3 -> x0, matrix products: 16 us -> none  [the longest x1 14.1 us: local(): jnp.dot(flattened, out_weight[0], preferred_element_type=jnp.float32)]
    ppermute x1 -> x30, waiting for transfers between devices: 1.52 us -> 16.8 us  [exchanged(): return lax.ppermute(array, ('section', 'tp'), pairs)]
    pallas_call x0 -> x4, Pallas kernels: none -> 14.6 us  [the longest x1 11.7 us: local(): pl.pallas_call(functools.partial(projection_kernel, tp, rows, heads, min(...]
    all_to_all x2 -> x0, waiting for transfers between devices: 13.7 us -> none  [the longest x1 8.08 us: local(): lax.all_to_all(levels, 'tp', split_axis=1, concat_axis=1, tiled=True)]
    add x15 -> x0, other arithmetic: 8.34 us -> none  [the longest x7 8.22 us: join_parts(): earlier[2] * factor_one[..., None] + later[2] * factor_two[..., None]]
  transfers between devices with their start and end apart: 4 -> 30, of which waited for: 3 -> 10; matrix products, arithmetic and copies ran while one was open for 18% -> 0% of each run, Pallas kernels for 0% -> 15%
where the time goes in v1:
time: 80.8 us; the launch traced here: 80.4 us
  starting transfers between devices  45.3 us (56%)
  waiting for transfers between devices  16.8 us (21%)
  Pallas kernels  14.6 us (18%)
  local copies, waits for them, and re-layouts  3.68 us (5%)
    ppermute x30, starting transfers between devices, exchanged(): return lax.ppermute(array, ('section', 'tp'), pairs)  45.3 us
    ppermute x30, waiting for transfers between devices, exchanged(): return lax.ppermute(array, ('section', 'tp'), pairs)  16.8 us
    pallas_call x1, Pallas kernels, local(): pl.pallas_call(functools.partial(projection_kernel, tp, rows, heads, min(...  11.7 us
    unnamed x8, local copies, waits for them, and re-layouts  3.68 us
    pallas_call x1, Pallas kernels, local(): pl.pallas_call(functools.partial(attention_kernel, tp, group), out_shape=...  2.05 us
  transfers between devices with their start and end apart: 30, of which 10 were waited for; matrix products, arithmetic and copies ran while one was open for 0% of the time, Pallas kernels for 15%

profile of v1, /device:TPU:0, one launch (start us, length us, event | category | flops | bytes accessed | tf_op | source)
XLA Modules:
  0.0 80.4 jit_solution(8656470913814198003)
XLA Ops:
  0.0 5.0 %collective-permute-start.6 = (bf16[1,8,8,128]{3,2,1,0:T(8,128)(2,1)}, bf16[1,8,8,128]{3,2,1,0:T(8,128)(2,1)S(1)}, u32[]{:S(2)}, u32[]{:S(2)}) collective-permute-start(bf16[1,8,8,128]{3,2,1,0:T(8,128)(2,1)} %refs_0_.1), channel_id=1, source_target_pairs={{0,6},{1,7},{2,4},{3,5},{4,2},{5,3},{6,0},{7,1},{8,14},{9,15},{10,... | collective-permute-start | bytes 49160 | tf_op jit(solution)/shard_map/ppermute | solution.py:25
  5.4 3.5 %collective-permute-start.4 = (bf16[1,8,8,128]{3,2,1,0:T(8,128)(2,1)}, bf16[1,8,8,128]{3,2,1,0:T(8,128)(2,1)S(1)}, u32[]{:S(2)}, u32[]{:S(2)}) collective-permute-start(bf16[1,8,8,128]{3,2,1,0:T(8,128)(2,1)} %refs_0_.1), channel_id=1, source_target_pairs={{0,4},{1,5},{2,6},{3,7},{4,0},{5,1},{6,2},{7,3},{8,12},{9,13},{10,... | collective-permute-start | bytes 49160 | tf_op jit(solution)/shard_map/ppermute | solution.py:25
  8.9 2.0 %collective-permute-start.2 = (bf16[1,8,8,128]{3,2,1,0:T(8,128)(2,1)}, bf16[1,8,8,128]{3,2,1,0:T(8,128)(2,1)S(1)}, u32[]{:S(2)}, u32[]{:S(2)}) collective-permute-start(bf16[1,8,8,128]{3,2,1,0:T(8,128)(2,1)} %refs_0_.1), channel_id=1, source_target_pairs={{0,2},{1,3},{2,0},{3,1},{4,6},{5,7},{6,4},{7,5},{8,10},{9,11},{10,... | collective-permute-start | bytes 49160 | tf_op jit(solution)/shard_map/ppermute | solution.py:25
  10.9 1.5 %collective-permute-start.1 = (bf16[1,8,8,128]{3,2,1,0:T(8,128)(2,1)}, bf16[1,8,8,128]{3,2,1,0:T(8,128)(2,1)S(1)}, u32[]{:S(2)}, u32[]{:S(2)}) collective-permute-start(bf16[1,8,8,128]{3,2,1,0:T(8,128)(2,1)} %refs_0_.1), channel_id=1, source_target_pairs={{0,1},{1,0},{2,3},{3,2},{4,5},{5,4},{6,7},{7,6},{8,9},{9,8},{10,11... | collective-permute-start | bytes 49160 | tf_op jit(solution)/shard_map/ppermute | solution.py:25
  12.4 1.3 %collective-permute-done.3.refs_3_ = bf16[1,8,8,128]{3,2,1,0:T(8,128)(2,1)S(1)} collective-permute-done((bf16[1,8,8,128]{3,2,1,0:T(8,128)(2,1)}, bf16[1,8,8,128]{3,2,1,0:T(8,128)(2,1)S(1)}, u32[]{:S(2)}, u32[]{:S(2)}) %collective-permute-start.3) | collective-permute-done | bytes 16416 | tf_op jit(solution)/shard_map/ppermute | solution.py:25
  14.9 4.2 %collective-permute-done.7.refs_7_ = bf16[1,8,8,128]{3,2,1,0:T(8,128)(2,1)S(1)} collective-permute-done((bf16[1,8,8,128]{3,2,1,0:T(8,128)(2,1)}, bf16[1,8,8,128]{3,2,1,0:T(8,128)(2,1)S(1)}, u32[]{:S(2)}, u32[]{:S(2)}) %collective-permute-start.7) | collective-permute-done | bytes 16416 | tf_op jit(solution)/shard_map/ppermute | solution.py:25
  19.1 1.6 %copy-done = bf16[1,8,2,4,128,128]{5,4,3,2,1,0:T(8,128)(2,1)S(1)} copy-done((bf16[1,8,2,4,128,128]{5,4,3,2,1,0:T(8,128)(2,1)S(1)}, bf16[1,8,2,4,128,128]{5,4,3,2,1,0:T(8,128)(2,1)}, u32[]{:S(2)}) %copy-start) | copy-done | bytes 2097176
  22.8 2.0 %attention.1 = (bf16[80,128]{1,0:T(8,128)(2,1)S(1)}, bf16[80,128]{1,0:T(8,128)(2,1)S(1)}, bf16[80,128]{1,0:T(8,128)(2,1)S(1)}, bf16[80,128]{1,0:T(8,128)(2,1)S(1...) custom-call(s32[1,8]{1,0:T(1,128)S(1)} %copy-done.3, ...), custom_call_target="tpu_custom_call" | custom-call | tf_op jit(solution)/shard_map/attention/pallas_call | solution.py:196
  25.4 3.0 %collective-permute-start.10 = (bf16[80,128]{1,0:T(8,128)(2,1)S(1)}, bf16[80,128]{1,0:T(8,128)(2,1)S(1)}, u32[]{:S(2)}, u32[]{:S(2)}) collective-permute-start(bf16[80,128]{1,0:T(8,128)(2,1)S(1)} %get-tuple-element.24), channel_id=1, source_target_pairs={{0,3},{1,2},{2,1},{3,0},{4,7},{5,6},{6,5},{7,4},{8,11},{9,10},{10,... | collective-permute-start | bytes 61448 | tf_op jit(solution)/shard_map/ppermute | solution.py:25
  28.4 2.9 %collective-permute-start.12 = (bf16[80,128]{1,0:T(8,128)(2,1)S(1)}, bf16[80,128]{1,0:T(8,128)(2,1)S(1)}, u32[]{:S(2)}, u32[]{:S(2)}) collective-permute-start(bf16[80,128]{1,0:T(8,128)(2,1)S(1)} %get-tuple-element.26), channel_id=1, source_target_pairs={{0,5},{1,4},{2,7},{3,6},{4,1},{5,0},{6,3},{7,2},{8,13},{9,12},{10,... | collective-permute-start | bytes 61448 | tf_op jit(solution)/shard_map/ppermute | solution.py:25
  31.3 4.7 %collective-permute-start.14 = (bf16[80,128]{1,0:T(8,128)(2,1)S(1)}, bf16[80,128]{1,0:T(8,128)(2,1)S(1)}, u32[]{:S(2)}, u32[]{:S(2)}) collective-permute-start(bf16[80,128]{1,0:T(8,128)(2,1)S(1)} %get-tuple-element.28), channel_id=1, source_target_pairs={{0,7},{1,6},{2,5},{3,4},{4,3},{5,2},{6,1},{7,0},{8,15},{9,14},{10,... | collective-permute-start | bytes 61448 | tf_op jit(solution)/shard_map/ppermute | solution.py:25
  38.0 11.7 %projection.1 = (bf16[8,2048]{1,0:T(8,128)(2,1)S(1)}, bf16[8,2048]{1,0:T(8,128)(2,1)S(1)}, bf16[8,2048]{1,0:T(8,128)(2,1)S(1)}, bf16[8,2048]{1,0:T(8,128)(2,1)S(...) custom-call(bf16[1,1024,16384]{2,1,0:T(8,128)(2,1)} %weight_ref.1, ...), custom_call_target="tpu_custom_call" | custom-call | tf_op jit(solution)/shard_map/projection/pallas_call | solution.py:206
  49.8 1.6 %collective-permute-start.16 = (bf16[8,2048]{1,0:T(8,128)(2,1)S(1)}, bf16[8,2048]{1,0:T(8,128)(2,1)S(1)}, u32[]{:S(2)}, u32[]{:S(2)}) collective-permute-start(bf16[8,2048]{1,0:T(8,128)(2,1)S(1)} %get-tuple-element.30), channel_id=1, source_target_pairs={{0,9},{1,8},{2,11},{3,10},{4,13},{5,12},{6,15},{7,14},{8,1},{9,0},... | collective-permute-start | bytes 98312 | tf_op jit(solution)/shard_map/ppermute | solution.py:25
  51.4 1.7 %collective-permute-start.18 = (bf16[8,2048]{1,0:T(8,128)(2,1)S(1)}, bf16[8,2048]{1,0:T(8,128)(2,1)S(1)}, u32[]{:S(2)}, u32[]{:S(2)}) collective-permute-start(bf16[8,2048]{1,0:T(8,128)(2,1)S(1)} %get-tuple-element.32), channel_id=1, source_target_pairs={{0,11},{1,10},{2,9},{3,8},{4,15},{5,14},{6,13},{7,12},{8,3},{9,2},... | collective-permute-start | bytes 98312 | tf_op jit(solution)/shard_map/ppermute | solution.py:25
  53.1 2.2 %collective-permute-start.19 = (bf16[8,2048]{1,0:T(8,128)(2,1)S(1)}, bf16[8,2048]{1,0:T(8,128)(2,1)S(1)}, u32[]{:S(2)}, u32[]{:S(2)}) collective-permute-start(bf16[8,2048]{1,0:T(8,128)(2,1)S(1)} %get-tuple-element.33), channel_id=1, source_target_pairs={{0,12},{1,13},{2,14},{3,15},{4,8},{5,9},{6,10},{7,11},{8,4},{9,5},... | collective-permute-start | bytes 98312 | tf_op jit(solution)/shard_map/ppermute | solution.py:25
  55.2 1.4 %collective-permute-start.20 = (bf16[8,2048]{1,0:T(8,128)(2,1)S(1)}, bf16[8,2048]{1,0:T(8,128)(2,1)S(1)}, u32[]{:S(2)}, u32[]{:S(2)}) collective-permute-start(bf16[8,2048]{1,0:T(8,128)(2,1)S(1)} %get-tuple-element.34), channel_id=1, source_target_pairs={{0,13},{1,12},{2,15},{3,14},{4,9},{5,8},{6,11},{7,10},{8,5},{9,4},... | collective-permute-start | bytes 98312 | tf_op jit(solution)/shard_map/ppermute | solution.py:25
  56.7 3.3 %collective-permute-start.21 = (bf16[8,2048]{1,0:T(8,128)(2,1)S(1)}, bf16[8,2048]{1,0:T(8,128)(2,1)S(1)}, u32[]{:S(2)}, u32[]{:S(2)}) collective-permute-start(bf16[8,2048]{1,0:T(8,128)(2,1)S(1)} %get-tuple-element.35), channel_id=1, source_target_pairs={{0,14},{1,15},{2,12},{3,13},{4,10},{5,11},{6,8},{7,9},{8,6},{9,7},... | collective-permute-start | bytes 98312 | tf_op jit(solution)/shard_map/ppermute | solution.py:25
  60.5 1.6 %collective-permute-done.21.refs_6_ = bf16[8,2048]{1,0:T(8,128)(2,1)S(1)} collective-permute-done((bf16[8,2048]{1,0:T(8,128)(2,1)S(1)}, bf16[8,2048]{1,0:T(8,128)(2,1)S(1)}, u32[]{:S(2)}, u32[]{:S(2)}) %collective-permute-start.21) | collective-permute-done | bytes 32800 | tf_op jit(solution)/shard_map/ppermute | solution.py:25
  62.1 3.9 %collective-permute-done.22.refs_7_ = bf16[8,2048]{1,0:T(8,128)(2,1)S(1)} collective-permute-done((bf16[8,2048]{1,0:T(8,128)(2,1)S(1)}, bf16[8,2048]{1,0:T(8,128)(2,1)S(1)}, u32[]{:S(2)}, u32[]{:S(2)}) %collective-permute-start.22) | collective-permute-done | bytes 32800 | tf_op jit(solution)/shard_map/ppermute | solution.py:25
  67.3 2.6 %collective-permute-start.28 = (bf16[8,2048]{1,0:T(8,128)(2,1)S(1)}, bf16[8,2048]{1,0:T(8,128)(2,1)S(1)}, u32[]{:S(2)}, u32[]{:S(2)}) collective-permute-start(bf16[8,2048]{1,0:T(8,128)(2,1)S(1)} %owner_sum.1.refs_0_), channel_id=1, source_target_pairs={{0,6},{1,7},{2,4},{3,5},{4,2},{5,3},{6,0},{7,1},{8,14},{9,15},{10,... | collective-permute-start | bytes 98312 | tf_op jit(solution)/shard_map/ppermute | solution.py:25
  69.9 3.9 %collective-permute-start.26 = (bf16[8,2048]{1,0:T(8,128)(2,1)S(1)}, bf16[8,2048]{1,0:T(8,128)(2,1)S(1)}, u32[]{:S(2)}, u32[]{:S(2)}) collective-permute-start(bf16[8,2048]{1,0:T(8,128)(2,1)S(1)} %owner_sum.1.refs_0_), channel_id=1, source_target_pairs={{0,4},{1,5},{2,6},{3,7},{4,0},{5,1},{6,2},{7,3},{8,12},{9,13},{10,... | collective-permute-start | bytes 98312 | tf_op jit(solution)/shard_map/ppermute | solution.py:25
  73.8 2.0 %collective-permute-start.24 = (bf16[8,2048]{1,0:T(8,128)(2,1)S(1)}, bf16[8,2048]{1,0:T(8,128)(2,1)S(1)}, u32[]{:S(2)}, u32[]{:S(2)}) collective-permute-start(bf16[8,2048]{1,0:T(8,128)(2,1)S(1)} %owner_sum.1.refs_0_), channel_id=1, source_target_pairs={{0,2},{1,3},{2,0},{3,1},{4,6},{5,7},{6,4},{7,5},{8,10},{9,11},{10,... | collective-permute-start | bytes 98312 | tf_op jit(solution)/shard_map/ppermute | solution.py:25
  75.8 1.5 %collective-permute-start.23 = (bf16[8,2048]{1,0:T(8,128)(2,1)S(1)}, bf16[8,2048]{1,0:T(8,128)(2,1)S(1)}, u32[]{:S(2)}, u32[]{:S(2)}) collective-permute-start(bf16[8,2048]{1,0:T(8,128)(2,1)S(1)} %owner_sum.1.refs_0_), channel_id=1, source_target_pairs={{0,1},{1,0},{2,3},{3,2},{4,5},{5,4},{6,7},{7,6},{8,9},{9,8},{10,11... | collective-permute-start | bytes 98312 | tf_op jit(solution)/shard_map/ppermute | solution.py:25
  77.3 1.3 %collective-permute-done.25.refs_3_ = bf16[8,2048]{1,0:T(8,128)(2,1)S(1)} collective-permute-done((bf16[8,2048]{1,0:T(8,128)(2,1)S(1)}, bf16[8,2048]{1,0:T(8,128)(2,1)S(1)}, u32[]{:S(2)}, u32[]{:S(2)}) %collective-permute-start.25) | collective-permute-done | bytes 32800 | tf_op jit(solution)/shard_map/ppermute | solution.py:25
  (48 shorter events, 10.0 us)
Async XLA Ops:
  0.0 10.9 %collective-permute-start.6 = (bf16[1,8,8,128]{3,2,1,0:T(8,128)(2,1)}, bf16[1,8,8,128]{3,2,1,0:T(8,128)(2,1)S(1)}, u32[]{:S(2)}, u32[]{:S(2)}) collective-permute-start(bf16[1,8,8,128]{3,2,1,0:T(8,128)(2,1)} %refs_0_.1), channel_id=1, source_target_pairs={{0,6},{1,7},{2,4},{3,5},{4,2},{5,3},{6,0},{7,1},{8,14},{9,15},{10,... | collective-permute-start | bytes 49160 | tf_op jit(solution)/shard_map/ppermute | solution.py:25
  5.0 7.4 %collective-permute-start.5 = (bf16[1,8,8,128]{3,2,1,0:T(8,128)(2,1)}, bf16[1,8,8,128]{3,2,1,0:T(8,128)(2,1)S(1)}, u32[]{:S(2)}, u32[]{:S(2)}) collective-permute-start(bf16[1,8,8,128]{3,2,1,0:T(8,128)(2,1)} %refs_0_.1), channel_id=1, source_target_pairs={{0,5},{1,4},{2,7},{3,6},{4,1},{5,0},{6,3},{7,2},{8,13},{9,12},{10,... | collective-permute-start | bytes 49160 | tf_op jit(solution)/shard_map/ppermute | solution.py:25
  5.4 7.0 %collective-permute-start.4 = (bf16[1,8,8,128]{3,2,1,0:T(8,128)(2,1)}, bf16[1,8,8,128]{3,2,1,0:T(8,128)(2,1)S(1)}, u32[]{:S(2)}, u32[]{:S(2)}) collective-permute-start(bf16[1,8,8,128]{3,2,1,0:T(8,128)(2,1)} %refs_0_.1), channel_id=1, source_target_pairs={{0,4},{1,5},{2,6},{3,7},{4,0},{5,1},{6,2},{7,3},{8,12},{9,13},{10,... | collective-permute-start | bytes 49160 | tf_op jit(solution)/shard_map/ppermute | solution.py:25
  12.4 6.6 %collective-permute-start.7 = (bf16[1,8,8,128]{3,2,1,0:T(8,128)(2,1)}, bf16[1,8,8,128]{3,2,1,0:T(8,128)(2,1)S(1)}, u32[]{:S(2)}, u32[]{:S(2)}) collective-permute-start(bf16[1,8,8,128]{3,2,1,0:T(8,128)(2,1)} %refs_0_.1), channel_id=1, source_target_pairs={{0,7},{1,6},{2,5},{3,4},{4,3},{5,2},{6,1},{7,0},{8,15},{9,14},{10,... | collective-permute-start | bytes 49160 | tf_op jit(solution)/shard_map/ppermute | solution.py:25
  24.8 6.4 %collective-permute-start.8 = (bf16[80,128]{1,0:T(8,128)(2,1)S(1)}, bf16[80,128]{1,0:T(8,128)(2,1)S(1)}, u32[]{:S(2)}, u32[]{:S(2)}) collective-permute-start(bf16[80,128]{1,0:T(8,128)(2,1)S(1)} %get-tuple-element.22), channel_id=1, source_target_pairs={{0,1},{1,0},{2,3},{3,2},{4,5},{5,4},{6,7},{7,6},{8,9},{9,8},{10,11... | collective-permute-start | bytes 61448 | tf_op jit(solution)/shard_map/ppermute | solution.py:25
  25.4 5.9 %collective-permute-start.9 = (bf16[80,128]{1,0:T(8,128)(2,1)S(1)}, bf16[80,128]{1,0:T(8,128)(2,1)S(1)}, u32[]{:S(2)}, u32[]{:S(2)}) collective-permute-start(bf16[80,128]{1,0:T(8,128)(2,1)S(1)} %get-tuple-element.23), channel_id=1, source_target_pairs={{0,2},{1,3},{2,0},{3,1},{4,6},{5,7},{6,4},{7,5},{8,10},{9,11},{10,... | collective-permute-start | bytes 61448 | tf_op jit(solution)/shard_map/ppermute | solution.py:25
  25.4 10.6 %collective-permute-start.10 = (bf16[80,128]{1,0:T(8,128)(2,1)S(1)}, bf16[80,128]{1,0:T(8,128)(2,1)S(1)}, u32[]{:S(2)}, u32[]{:S(2)}) collective-permute-start(bf16[80,128]{1,0:T(8,128)(2,1)S(1)} %get-tuple-element.24), channel_id=1, source_target_pairs={{0,3},{1,2},{2,1},{3,0},{4,7},{5,6},{6,5},{7,4},{8,11},{9,10},{10,... | collective-permute-start | bytes 61448 | tf_op jit(solution)/shard_map/ppermute | solution.py:25
  28.4 7.7 %collective-permute-start.11 = (bf16[80,128]{1,0:T(8,128)(2,1)S(1)}, bf16[80,128]{1,0:T(8,128)(2,1)S(1)}, u32[]{:S(2)}, u32[]{:S(2)}) collective-permute-start(bf16[80,128]{1,0:T(8,128)(2,1)S(1)} %get-tuple-element.25), channel_id=1, source_target_pairs={{0,4},{1,5},{2,6},{3,7},{4,0},{5,1},{6,2},{7,3},{8,12},{9,13},{10,... | collective-permute-start | bytes 61448 | tf_op jit(solution)/shard_map/ppermute | solution.py:25
  28.4 7.7 %collective-permute-start.12 = (bf16[80,128]{1,0:T(8,128)(2,1)S(1)}, bf16[80,128]{1,0:T(8,128)(2,1)S(1)}, u32[]{:S(2)}, u32[]{:S(2)}) collective-permute-start(bf16[80,128]{1,0:T(8,128)(2,1)S(1)} %get-tuple-element.26), channel_id=1, source_target_pairs={{0,5},{1,4},{2,7},{3,6},{4,1},{5,0},{6,3},{7,2},{8,13},{9,12},{10,... | collective-permute-start | bytes 61448 | tf_op jit(solution)/shard_map/ppermute | solution.py:25
  31.2 5.6 %collective-permute-start.13 = (bf16[80,128]{1,0:T(8,128)(2,1)S(1)}, bf16[80,128]{1,0:T(8,128)(2,1)S(1)}, u32[]{:S(2)}, u32[]{:S(2)}) collective-permute-start(bf16[80,128]{1,0:T(8,128)(2,1)S(1)} %get-tuple-element.27), channel_id=1, source_target_pairs={{0,6},{1,7},{2,4},{3,5},{4,2},{5,3},{6,0},{7,1},{8,14},{9,15},{10,... | collective-permute-start | bytes 61448 | tf_op jit(solution)/shard_map/ppermute | solution.py:25
  31.3 6.7 %collective-permute-start.14 = (bf16[80,128]{1,0:T(8,128)(2,1)S(1)}, bf16[80,128]{1,0:T(8,128)(2,1)S(1)}, u32[]{:S(2)}, u32[]{:S(2)}) collective-permute-start(bf16[80,128]{1,0:T(8,128)(2,1)S(1)} %get-tuple-element.28), channel_id=1, source_target_pairs={{0,7},{1,6},{2,5},{3,4},{4,3},{5,2},{6,1},{7,0},{8,15},{9,14},{10,... | collective-permute-start | bytes 61448 | tf_op jit(solution)/shard_map/ppermute | solution.py:25
  36.0 17.1 %collective-permute-start = (bf16[1,8,2048]{2,1,0:T(8,128)(2,1)}, bf16[1,8,2048]{2,1,0:T(8,128)(2,1)S(1)}, u32[]{:S(2)}, u32[]{:S(2)}) collective-permute-start(bf16[1,8,2048]{2,1,0:T(8,128)(2,1)} %param.10), channel_id=1, source_target_pairs={{0,8},{1,9},{2,10},{3,11},{4,12},{5,13},{6,14},{7,15},{8,0},{9,1},... | collective-permute-start | bytes 98312 | tf_op jit(solution)/shard_map/ppermute | solution.py:25
  49.7 5.6 %collective-permute-start.15 = (bf16[8,2048]{1,0:T(8,128)(2,1)S(1)}, bf16[8,2048]{1,0:T(8,128)(2,1)S(1)}, u32[]{:S(2)}, u32[]{:S(2)}) collective-permute-start(bf16[8,2048]{1,0:T(8,128)(2,1)S(1)} %get-tuple-element.29), channel_id=1, source_target_pairs={{0,8},{1,9},{2,10},{3,11},{4,12},{5,13},{6,14},{7,15},{8,0},{9,1},... | collective-permute-start | bytes 98312 | tf_op jit(solution)/shard_map/ppermute | solution.py:25
  49.8 6.9 %collective-permute-start.16 = (bf16[8,2048]{1,0:T(8,128)(2,1)S(1)}, bf16[8,2048]{1,0:T(8,128)(2,1)S(1)}, u32[]{:S(2)}, u32[]{:S(2)}) collective-permute-start(bf16[8,2048]{1,0:T(8,128)(2,1)S(1)} %get-tuple-element.30), channel_id=1, source_target_pairs={{0,9},{1,8},{2,11},{3,10},{4,13},{5,12},{6,15},{7,14},{8,1},{9,0},... | collective-permute-start | bytes 98312 | tf_op jit(solution)/shard_map/ppermute | solution.py:25
  51.4 8.6 %collective-permute-start.17 = (bf16[8,2048]{1,0:T(8,128)(2,1)S(1)}, bf16[8,2048]{1,0:T(8,128)(2,1)S(1)}, u32[]{:S(2)}, u32[]{:S(2)}) collective-permute-start(bf16[8,2048]{1,0:T(8,128)(2,1)S(1)} %get-tuple-element.31), channel_id=1, source_target_pairs={{0,10},{1,11},{2,8},{3,9},{4,14},{5,15},{6,12},{7,13},{8,2},{9,3},... | collective-permute-start | bytes 98312 | tf_op jit(solution)/shard_map/ppermute | solution.py:25
  51.4 8.8 %collective-permute-start.18 = (bf16[8,2048]{1,0:T(8,128)(2,1)S(1)}, bf16[8,2048]{1,0:T(8,128)(2,1)S(1)}, u32[]{:S(2)}, u32[]{:S(2)}) collective-permute-start(bf16[8,2048]{1,0:T(8,128)(2,1)S(1)} %get-tuple-element.32), channel_id=1, source_target_pairs={{0,11},{1,10},{2,9},{3,8},{4,15},{5,14},{6,13},{7,12},{8,3},{9,2},... | collective-permute-start | bytes 98312 | tf_op jit(solution)/shard_map/ppermute | solution.py:25
  53.1 7.1 %collective-permute-start.19 = (bf16[8,2048]{1,0:T(8,128)(2,1)S(1)}, bf16[8,2048]{1,0:T(8,128)(2,1)S(1)}, u32[]{:S(2)}, u32[]{:S(2)}) collective-permute-start(bf16[8,2048]{1,0:T(8,128)(2,1)S(1)} %get-tuple-element.33), channel_id=1, source_target_pairs={{0,12},{1,13},{2,14},{3,15},{4,8},{5,9},{6,10},{7,11},{8,4},{9,5},... | collective-permute-start | bytes 98312 | tf_op jit(solution)/shard_map/ppermute | solution.py:25
  55.2 5.2 %collective-permute-start.20 = (bf16[8,2048]{1,0:T(8,128)(2,1)S(1)}, bf16[8,2048]{1,0:T(8,128)(2,1)S(1)}, u32[]{:S(2)}, u32[]{:S(2)}) collective-permute-start(bf16[8,2048]{1,0:T(8,128)(2,1)S(1)} %get-tuple-element.34), channel_id=1, source_target_pairs={{0,13},{1,12},{2,15},{3,14},{4,9},{5,8},{6,11},{7,10},{8,5},{9,4},... | collective-permute-start | bytes 98312 | tf_op jit(solution)/shard_map/ppermute | solution.py:25
  56.7 5.4 %collective-permute-start.21 = (bf16[8,2048]{1,0:T(8,128)(2,1)S(1)}, bf16[8,2048]{1,0:T(8,128)(2,1)S(1)}, u32[]{:S(2)}, u32[]{:S(2)}) collective-permute-start(bf16[8,2048]{1,0:T(8,128)(2,1)S(1)} %get-tuple-element.35), channel_id=1, source_target_pairs={{0,14},{1,15},{2,12},{3,13},{4,10},{5,11},{6,8},{7,9},{8,6},{9,7},... | collective-permute-start | bytes 98312 | tf_op jit(solution)/shard_map/ppermute | solution.py:25
  59.9 6.0 %collective-permute-start.22 = (bf16[8,2048]{1,0:T(8,128)(2,1)S(1)}, bf16[8,2048]{1,0:T(8,128)(2,1)S(1)}, u32[]{:S(2)}, u32[]{:S(2)}) collective-permute-start(bf16[8,2048]{1,0:T(8,128)(2,1)S(1)} %get-tuple-element.36), channel_id=1, source_target_pairs={{0,15},{1,14},{2,13},{3,12},{4,11},{5,10},{6,9},{7,8},{8,7},{9,6},... | collective-permute-start | bytes 98312 | tf_op jit(solution)/shard_map/ppermute | solution.py:25
  66.1 7.7 %collective-permute-start.29 = (bf16[8,2048]{1,0:T(8,128)(2,1)S(1)}, bf16[8,2048]{1,0:T(8,128)(2,1)S(1)}, u32[]{:S(2)}, u32[]{:S(2)}) collective-permute-start(bf16[8,2048]{1,0:T(8,128)(2,1)S(1)} %owner_sum.1.refs_0_), channel_id=1, source_target_pairs={{0,7},{1,6},{2,5},{3,4},{4,3},{5,2},{6,1},{7,0},{8,15},{9,14},{10,... | collective-permute-start | bytes 98312 | tf_op jit(solution)/shard_map/ppermute | solution.py:25
  67.3 8.5 %collective-permute-start.28 = (bf16[8,2048]{1,0:T(8,128)(2,1)S(1)}, bf16[8,2048]{1,0:T(8,128)(2,1)S(1)}, u32[]{:S(2)}, u32[]{:S(2)}) collective-permute-start(bf16[8,2048]{1,0:T(8,128)(2,1)S(1)} %owner_sum.1.refs_0_), channel_id=1, source_target_pairs={{0,6},{1,7},{2,4},{3,5},{4,2},{5,3},{6,0},{7,1},{8,14},{9,15},{10,... | collective-permute-start | bytes 98312 | tf_op jit(solution)/shard_map/ppermute | solution.py:25
  69.9 7.4 %collective-permute-start.27 = (bf16[8,2048]{1,0:T(8,128)(2,1)S(1)}, bf16[8,2048]{1,0:T(8,128)(2,1)S(1)}, u32[]{:S(2)}, u32[]{:S(2)}) collective-permute-start(bf16[8,2048]{1,0:T(8,128)(2,1)S(1)} %owner_sum.1.refs_0_), channel_id=1, source_target_pairs={{0,5},{1,4},{2,7},{3,6},{4,1},{5,0},{6,3},{7,2},{8,13},{9,12},{10,... | collective-permute-start | bytes 98312 | tf_op jit(solution)/shard_map/ppermute | solution.py:25
  69.9 7.4 %collective-permute-start.26 = (bf16[8,2048]{1,0:T(8,128)(2,1)S(1)}, bf16[8,2048]{1,0:T(8,128)(2,1)S(1)}, u32[]{:S(2)}, u32[]{:S(2)}) collective-permute-start(bf16[8,2048]{1,0:T(8,128)(2,1)S(1)} %owner_sum.1.refs_0_), channel_id=1, source_target_pairs={{0,4},{1,5},{2,6},{3,7},{4,0},{5,1},{6,2},{7,3},{8,12},{9,13},{10,... | collective-permute-start | bytes 98312 | tf_op jit(solution)/shard_map/ppermute | solution.py:25
  (10 other events, 30.9 us)
